TPU v7x, 256 devices: a whole 4x4x8 slice. The times are simulated.
256 devices in a mesh: lat: 16 (over y, x), lon: 16 (over z, core).
Axes of the slice: x: 4, y: 4, z: 8, core: 2. Of those that a mesh axis runs over, the one named last changes fastest.
Arguments:
- grid: bfloat16 [512, 4096, 128], P('lat', 'lon'), may hold values from -6 to 6
- npts: int32 [512], replicated, may hold values from 3328 to 4096, as said below
- fraction: bfloat16 [512, 4096], P('lat', 'lon'), may hold values from 0 to 1
- start: int32 [512, 4096], P('lat', 'lon'), may hold values from 0 to 124
- src_dev: int32 [16, 16, 64, 1], P('lat', 'lon'), may hold values from 0 to 15; in each aligned block of 64 rows (0 to 63, 64 to 127, ..., all dimensions but the last counted through in order) at most 8 rows name the same one
- src_sub: int32 [16, 16, 64], P('lat', 'lon'), may hold values from 0 to 1
Outputs:
- departed: bfloat16 [512, 4096, 128], P('lat', 'lon')
- fourier: float32 [512, 2, 1280, 128], P(('lat', 'lon'))
Inputs may be any that keep to these rules, and one draw needn't show every extreme that they name: `npts`: each a multiple of 4; one latitude has exactly 4096 points and one exactly the least value. `src_dev`: among the 64 arrival blocks of one device no sector is named by more than 8 of them; some sector is named by exactly 8. `start`: the four stencil points lie inside the source block.
All inputs are finite; a program needn't handle non-finite values.
Results may differ from a plain program's by a relative error of at most 0.0055.
Values may be sent and summed in bfloat16 or wider, within the bound.
A program may use at most 64 MiB of HBM per device.

v0:
```python
import math

import jax
import jax.numpy as jnp
from jax import lax
from jax.sharding import PartitionSpec as P

MMAX = 1280


def cubic_weights(shifted):
    return jnp.stack(
        [
            -shifted * (shifted - 1.0) * (shifted - 2.0) / 6.0,
            (shifted + 1.0) * (shifted - 1.0) * (shifted - 2.0) / 2.0,
            -(shifted + 1.0) * shifted * (shifted - 2.0) / 2.0,
            (shifted + 1.0) * shifted * (shifted - 1.0) / 6.0,
        ],
        axis=-1,
    )


def interpolate(table_rows, first, weights):
    window = first[:, None] + jnp.arange(4, dtype=jnp.int32)[None, :]
    picked = jnp.take(table_rows, window, axis=0)
    total = jnp.zeros((first.shape[0], table_rows.shape[1]), jnp.float32)
    for offset in range(4):
        total = total + weights[:, offset : offset + 1] * picked[:, offset, :].astype(jnp.float32)
    return total


def spectral(rows, counts):
    row_length = rows.shape[1]
    channels = rows.shape[2]
    block_waves = math.gcd(MMAX, 256)
    inner_width = 64
    outer_width = row_length // inner_width
    outer_ids = jnp.arange(outer_width, dtype=jnp.int32) * inner_width
    inner_ids = jnp.arange(inner_width, dtype=jnp.int32)

    def one_latitude(items):
        values, length = items
        step_angle = jnp.float32(2.0 * math.pi) / length.astype(jnp.float32)

        def one_block(block_index):
            wave_ids = block_index * block_waves + jnp.arange(block_waves, dtype=jnp.int32)
            outer_phase = (wave_ids[:, None] * outer_ids[None, :] % length).astype(
                jnp.float32
            ) * step_angle
            inner_phase = (wave_ids[:, None] * inner_ids[None, :] % length).astype(
                jnp.float32
            ) * step_angle
            outer_cos = jnp.cos(outer_phase)[:, :, None]
            outer_sin = jnp.sin(outer_phase)[:, :, None]
            inner_cos = jnp.cos(inner_phase)[:, None, :]
            inner_sin = jnp.sin(inner_phase)[:, None, :]
            cosine = (outer_cos * inner_cos - outer_sin * inner_sin).reshape(
                block_waves, row_length
            )
            sine = -(outer_sin * inner_cos + outer_cos * inner_sin).reshape(block_waves, row_length)
            table = jnp.concatenate([cosine, sine], axis=0)
            upper = table.astype(jnp.bfloat16)
            lower = (table - upper.astype(jnp.float32)).astype(jnp.bfloat16)
            result = jnp.dot(upper, values, preferred_element_type=jnp.float32)
            result = result + jnp.dot(lower, values, preferred_element_type=jnp.float32)
            return result.reshape(2, block_waves, channels)

        pieces = lax.map(one_block, jnp.arange(MMAX // block_waves, dtype=jnp.int32))
        joined = pieces.transpose(1, 0, 2, 3).reshape(2, MMAX, channels)
        return joined / jnp.sqrt(length.astype(jnp.float32))

    return lax.map(one_latitude, (rows, counts))


def per_device(grid, npts, fraction, start, src_dev, src_sub):
    lat_dev, lon_dev, channels = grid.shape
    groups = lax.axis_size("lon")
    lat_each = lat_dev // groups
    sub_blocks = lon_dev // 128
    block_total = lat_dev * sub_blocks
    band = lax.axis_index("lat")
    sector = lax.axis_index("lon")
    counts_band = lax.dynamic_slice_in_dim(npts, band * lat_dev, lat_dev)
    my_counts = lax.dynamic_slice_in_dim(counts_band, sector * lat_each, lat_each)
    column_ids = sector * lon_dev + jnp.arange(lon_dev, dtype=jnp.int32)
    live = (column_ids[None, :] < counts_band[:, None])[..., None]
    masked = jnp.where(live, grid, jnp.zeros_like(grid))
    dev_list = src_dev.reshape(block_total)
    sub_list = src_sub.reshape(block_total)
    slot_count = max(2, 2 * block_total // groups)
    everyone = (
        lax.all_gather(dev_list, "lon", axis=0, tiled=True),
        lax.all_gather(sub_list, "lon", axis=0, tiled=True),
    )
    all_dev = everyone[0].reshape(groups, block_total)
    all_sub = everyone[1].reshape(groups, block_total)
    hits = all_dev == sector
    rank = jnp.cumsum(hits.astype(jnp.int32), axis=1) - 1
    owner_block = (jnp.arange(block_total, dtype=jnp.int32) // sub_blocks)[
        None, :
    ] * sub_blocks + all_sub
    slot_ids = jnp.arange(slot_count, dtype=jnp.int32)
    chosen = hits[:, None, :] & (rank[:, None, :] == slot_ids[None, :, None])
    send_index = jnp.sum(jnp.where(chosen, owner_block[:, None, :], 0), axis=2)
    blocks = masked.reshape(block_total, 128, channels)
    outgoing = jnp.take(blocks, send_index.reshape(-1), axis=0).reshape(
        groups, slot_count, 128, channels
    )
    incoming = lax.all_to_all(outgoing, "lon", split_axis=0, concat_axis=0, tiled=True)
    own_hits = dev_list[None, :] == jnp.arange(groups, dtype=jnp.int32)[:, None]
    own_rank = jnp.cumsum(own_hits.astype(jnp.int32), axis=1) - 1
    my_rank = jnp.sum(jnp.where(own_hits, own_rank, 0), axis=0)
    slot_of_block = dev_list * slot_count + my_rank
    slot_points = jnp.repeat(slot_of_block.reshape(lat_dev, sub_blocks), 128, axis=1)
    first = slot_points * 128 + start
    weights = cubic_weights(fraction.astype(jnp.float32))
    flat_rows = incoming.reshape(groups * slot_count * 128, channels)
    values = interpolate(flat_rows, first.reshape(-1), weights.reshape(-1, 4)).reshape(
        lat_dev, lon_dev, channels
    )
    departed = jnp.where(live, values, jnp.zeros_like(values)).astype(jnp.bfloat16)
    rows = lax.all_to_all(departed, "lon", split_axis=0, concat_axis=1, tiled=True)
    fourier = spectral(rows, my_counts)
    return (departed, fourier)


def solution(mesh):
    in_specs = (
        P("lat", "lon", None),
        P(),
        P("lat", "lon"),
        P("lat", "lon"),
        P("lat", "lon", None, None),
        P("lat", "lon", None),
    )
    out_specs = (P("lat", "lon", None), P(("lat", "lon"), None, None, None))
    return jax.shard_map(
        per_device, mesh=mesh, in_specs=in_specs, out_specs=out_specs, check_vma=False
    )
```

profile of v0, /device:TPU:65, one launch (start us, length us, event | category | flops | bytes accessed | tf_op | source)
XLA Modules:
  0.0 423.7 jit_solution(8886235945282636476)
XLA Ops:
  4.1 12.2 %all-reduce.2 = (s32[1024]{0:T(1024)S(1)}, s32[1024]{0:T(1024)S(1)}) all-reduce(s32[1024]{0:T(1024)S(1)} %bitcast_dynamic-update-slice_fusion, s32[1024]{0:T(1024)S(1)} %bitcast_dynamic-update-slice_fusion.1), channel_id=3, replica_groups=mesh['lat'=16,'lon'=16] {'lon'}, use_global_device_ids=true, to_apply=%add.1 | all-reduce | flops 2048 | bytes 16384
  18.1 3.2 broadcast_select_fusion.2
  21.3 3.0 gather_fusion
  24.3 4.6 %broadcast_select_fusion.1 = bf16[16,8,128,128]{3,2,1,0:T(8,128)(2,1)} fusion(bf16[16,8,128,128]{3,2,1,0:T(8,128)(2,1)} %bitcast.94, pred[16,8]{1,0:T(8,128)(4,1)S(1)} %compare_and_fusion), kind=kLoop, calls=%fused_computation.55 | loop fusion | flops 2097152 | bytes 8388736 | tf_op jit(solution)/shard_map/jit(_take)/select_n | solution.py:106
  28.9 8.6 %all-to-all-start = ((bf16[16,8,128,128]{3,2,1,0:T(8,128)(2,1)}), bf16[16,8,128,128]{3,2,1,0:T(8,128)(2,1)}, u32[]{:S(2)}, u32[]{:S(2)}) async-start(bf16[16,8,128,128]{3,2,1,0:T(8,128)(2,1)} %broadcast_select_fusion.1), calls=%async_computation | async-start | bytes 8388608 | tf_op jit(solution)/shard_map/all_to_all | solution.py:109
  38.2 5.1 %compare_select_fusion = s32[8192,4,1]{1,0,2:T(8,128)} fusion(s32[8192]{0:T(1024)S(1)} %bitcast.100), kind=kLoop, calls=%fused_computation.40 | loop fusion | flops 131072 | bytes 163840 | tf_op jit(solution)/shard_map/jit(_take)/jit(_where)/select_n | solution.py:25
  43.3 4.9 %reshape.444 = s32[32768]{0:T(1024)S(1)} reshape(s32[8192,4,1]{1,0,2:T(8,128)} %compare_select_fusion) | data formatting | bytes 262144 | tf_op jit(solution)/shard_map/jit(_take)/jit(_where)/select_n | solution.py:25
  48.2 1.7 copy.15
  50.0 80.2 %all-to-all-done = bf16[16,8,128,128]{3,2,1,0:T(8,128)(2,1)} async-done(((bf16[16,8,128,128]{3,2,1,0:T(8,128)(2,1)}), bf16[16,8,128,128]{3,2,1,0:T(8,128)(2,1)}, u32[]{:S(2)}, u32[]{:S(2)}) %all-to-all-start) | async-done | bytes 4194336 | tf_op jit(solution)/shard_map/all_to_all | solution.py:109
  130.2 112.9 %gather_fusion.1 = bf16[32768,128]{1,0:T(8,128)(2,1)} fusion(bf16[16384,128]{1,0:T(8,128)(2,1)} %bitcast.10, s32[32768]{0:T(1024)S(1)} %broadcast_clamp_fusion), kind=kCustom, calls=%fused_computation.1 | custom fusion | bytes 16908288 | tf_op jit(solution)/shard_map/jit(_take)/gather | solution.py:25
  243.1 25.9 %broadcast_select_fusion = bf16[8192,4,128]{2,1,0:T(4,128)(2,1)S(1)} fusion(bf16[8192,4,128]{2,1,0:T(4,128)(2,1)} %bitcast.91, pred[8192,4]{1,0:T(8,128)(4,1)S(1)} %copy.15), kind=kLoop, calls=%fused_computation.41 | loop fusion | flops 4194304 | bytes 16809984 | tf_op jit(solution)/shard_map/jit(_take)/select_n | solution.py:25
  269.0 11.6 %slice_convert_fusion.3 = (f32[8192,1,128]{2,1,0:T(1,128)S(1)}, f32[8192,1,128]{2,1,0:T(1,128)S(1)}, f32[8192,1,128]{2,1,0:T(1,128)S(1)}, f32[8192,1,128]{2,1,0:T(1,128)S(1)}) fusion(bf16[8192,4,128]{2,1,0:T(4,128)(2,1)S(1)} %broadcast_select_fusion), kind=kLoop, calls=%fused_computation.45 | loop fusion | flops 4194304 | bytes 25165824 | tf_op jit(solution)/shard_map/convert_element_type | solution.py:28
  280.7 7.7 %fusion.29 = bf16[32,256,128]{2,1,0:T(8,128)(2,1)} fusion(f32[32,256]{1,0:T(8,128)S(1)} %get-tuple-element.190, f32[32,256]{1,0:T(8,128)S(1)} %get-tuple-element.189, f32[32,256]{1,0:T(8,128)S(1)} %get-tuple-element.188, f32[32,256]{1,0:T(8,128)S(1)} %get-tuple-element.187, pred[32,256]{1,0:T(8,128)(4,1)S(1)} %broadcast_compare_fusion, ...), kind=kLoop, calls=%fused_computation.49 | loop fusion | flops 9437184 | bytes 19013632 | tf_op jit(solution)/shard_map/convert_element_type | solution.py:121
  288.4 6.5 %all-to-all-start.1 = ((bf16[32,256,128]{2,1,0:T(8,128)(2,1)}), bf16[32,256,128]{2,1,0:T(8,128)(2,1)S(1)}, u32[]{:S(2)}, u32[]{:S(2)}) async-start(bf16[32,256,128]{2,1,0:T(8,128)(2,1)} %fusion.29), calls=%async_computation.1 | async-start | bytes 4194304 | tf_op jit(solution)/shard_map/all_to_all | solution.py:122
  295.7 46.8 %all-to-all-done.1 = bf16[32,256,128]{2,1,0:T(8,128)(2,1)S(1)} async-done(((bf16[32,256,128]{2,1,0:T(8,128)(2,1)}), bf16[32,256,128]{2,1,0:T(8,128)(2,1)S(1)}, u32[]{:S(2)}, u32[]{:S(2)}) %all-to-all-start.1) | async-done | bytes 2097184 | tf_op jit(solution)/shard_map/all_to_all | solution.py:122
  342.4 1.3 copy-done.2
  343.8 1.7 copy.16
  345.5 78.2 %while.25 = (s32[]{:T(128)}, f32[2,2,1280,128]{3,2,1,0:T(8,128)}, s32[2]{0:T(128)S(1)}, bf16[2,4096,128]{2,1,0:T(8,128)(2,1)S(1)}, s32[]{:T(128)}, /*index=5*/s32[]{:T(128)}, f32[]{:T(128)}, s32[]{:T(128)}, s32[1]{0:T(128)}) while((s32[]{:T(128)}, f32[2,2,1280,128]{3,2,1,0:T(8,128)}, s32[2]{0:T(128)S(1)}, ...), condition=%wide.region_7.8_spmd.clone, body=%wide.region_4.7_spmd.clone.sunk | while | flops 1100677504 | bytes 55840748 | solution.py:72
  348.3 34.1 %while.26 = (s32[]{:T(128)}, f32[5,2,256,128]{3,2,1,0:T(8,128)S(1)}, s32[5]{0:T(128)S(1)}, s32[64]{0:T(128)S(1)}, s32[]{:T(128)}, /*index=5*/pred[]{:T(512)}, f3...) while((s32[]{:T(128)}, f32[5,2,256,128]{3,2,1,0:T(8,128)S(1)}, ...), condition=%wide.region_6.6_spmd, body=%wide.region_5.5_spmd.sunk | while | flops 1100349696 | bytes 29100692 | solution.py:68
  349.5 1.8 fusion.62
  356.3 1.8 fusion.62
  363.1 1.8 fusion.62
  367.4 1.3 fusion.64
  370.0 1.8 fusion.62
  376.8 1.8 fusion.62
  381.1 1.3 fusion.64
  387.4 34.1 %while.26 = (s32[]{:T(128)}, f32[5,2,256,128]{3,2,1,0:T(8,128)S(1)}, s32[5]{0:T(128)S(1)}, s32[64]{0:T(128)S(1)}, s32[]{:T(128)}, /*index=5*/pred[]{:T(512)}, f3...) while((s32[]{:T(128)}, f32[5,2,256,128]{3,2,1,0:T(8,128)S(1)}, ...), condition=%wide.region_6.6_spmd, body=%wide.region_5.5_spmd.sunk | while | flops 1100349696 | bytes 29100692 | solution.py:68
  388.6 1.8 fusion.62
  395.4 1.8 fusion.62
  402.2 1.8 fusion.62
  409.0 1.8 fusion.62
  415.9 1.8 fusion.62
  (126 shorter events, 53.0 us)
Async XLA Ops:
  28.9 8.6 %copy-start.5 = (s32[1,1,64,1]{2,3,1,0:T(1,128)S(1)}, s32[1,1,64,1]{2,3,1,0:T(1,128)}, u32[]{:S(2)}) copy-start(s32[1,1,64,1]{2,3,1,0:T(1,128)} %param.14) | copy-start | bytes 772
  28.9 9.3 %copy-start.3 = (s32[32,256]{1,0:T(8,128)S(1)}, s32[32,256]{1,0:T(8,128)}, u32[]{:S(2)}) copy-start(s32[32,256]{1,0:T(8,128)} %param.13) | copy-start | bytes 98308
  28.9 101.3 %all-to-all-start = ((bf16[16,8,128,128]{3,2,1,0:T(8,128)(2,1)}), bf16[16,8,128,128]{3,2,1,0:T(8,128)(2,1)}, u32[]{:S(2)}, u32[]{:S(2)}) async-start(bf16[16,8,128,128]{3,2,1,0:T(8,128)(2,1)} %broadcast_select_fusion.1), calls=%async_computation | async-start | bytes 8388608 | tf_op jit(solution)/shard_map/all_to_all | solution.py:109
  38.2 11.8 %copy-start.4 = (bf16[32,256]{1,0:T(8,128)(2,1)S(1)}, bf16[32,256]{1,0:T(8,128)(2,1)}, u32[]{:S(2)}) copy-start(bf16[32,256]{1,0:T(8,128)(2,1)} %param.12) | copy-start | bytes 49156
  288.4 54.0 %all-to-all-start.1 = ((bf16[32,256,128]{2,1,0:T(8,128)(2,1)}), bf16[32,256,128]{2,1,0:T(8,128)(2,1)S(1)}, u32[]{:S(2)}, u32[]{:S(2)}) async-start(bf16[32,256,128]{2,1,0:T(8,128)(2,1)} %fusion.29), calls=%async_computation.1 | async-start | bytes 4194304 | tf_op jit(solution)/shard_map/all_to_all | solution.py:122
  342.4 1.3 copy-start.2
  345.5 2.8 copy-start
  382.6 2.1 copy-start.1
  384.6 2.7 copy-start
  421.7 2.1 copy-start.1
where the time goes:
time: 427 us; the launch traced here: 424 us
  local copies, waits for them, and re-layouts  142 us (33%)
  waiting for transfers between devices  127 us (30%)
  other arithmetic  89.5 us (21%)
  matrix products  25.8 us (6%)
  starting transfers between devices  15.1 us (4%)
  blocking collectives  12.2 us (3%)
  loops' own time  10.3 us (2%)
    gather x1, local copies, waits for them, and re-layouts, interpolate(): picked = jnp.take(table_rows, window, axis=0)  113 us
    all_to_all x1, waiting for transfers between devices, per_device(): lax.all_to_all(outgoing, 'lon', split_axis=0, concat_axis=0, tiled=True)  80.2 us
    all_to_all x1, waiting for transfers between devices, per_device(): lax.all_to_all(departed, 'lon', split_axis=0, concat_axis=1, tiled=True)  46.8 us
    select_n x2, other arithmetic, interpolate(): picked = jnp.take(table_rows, window, axis=0)  31 us
    cos x10, other arithmetic, one_block(): outer_cos = jnp.cos(outer_phase)[:, :, None]  18.4 us
    dot_general x10, matrix products, one_block(): result = result + jnp.dot(lower, values, preferred_element_type=jnp.float32)  13 us
    dot_general x10, matrix products, one_block(): result = jnp.dot(upper, values, preferred_element_type=jnp.float32)  12.8 us
    unnamed x1, blocking collectives  12.2 us
  transfers between devices with their start and end apart: 2, of which 2 were waited for; matrix products, arithmetic and copies ran while one was open for 3% of the time, Pallas kernels for 0%

commit v1 on v0

v1 whole, which is shorter than its diff:
```python
import functools
import math

import jax
import jax.numpy as jnp
from jax import lax
from jax.experimental import pallas as pl
from jax.experimental.pallas import tpu as pltpu
from jax.sharding import PartitionSpec as P

MMAX = 1280
BLK = 128
WAVES = 128
INNER = 512
LEAST = 3328
FIX = float(1 << 24)
MESH = pl.DeviceIdType.MESH


def unit(turns):
    x = turns * math.pi
    y = x * x
    sine = x * (1.0 + y * (-1 / 6 + y * (1 / 120 + y * (-1 / 5040 + y * (1 / 362880 - y / 39916800)))))
    cosine = 1.0 + y * (
        -1 / 2 + y * (1 / 24 + y * (-1 / 720 + y * (1 / 40320 + y * (-1 / 3628800 + y / 479001600))))
    )
    return 1.0 - 2.0 * sine * sine, -2.0 * sine * cosine


def times(a, b):
    return a[0] * b[0] - a[1] * b[1], a[0] * b[1] + a[1] * b[0]


def turned(product, length, inverse):
    rest = product - jnp.round(product * inverse) * length
    return unit(rest * inverse)


def kernel(
    groups,
    npts,
    dev,
    sub,
    start,
    fraction,
    grid,
    departed,
    fourier,
    rows,
    moved,
    wide,
    table,
    spectrum,
    start_v,
    frac_v,
    frac_i,
    meta_out,
    meta_in,
    meta_s,
    send1,
    recv1,
    send_m,
    recv_m,
    send2,
    recv2,
    early,
    local,
):
    me = lax.axis_index("lon")
    band = lax.axis_index("lat")
    per = len(rows)
    lats = grid.shape[0]
    halves = grid.shape[1]
    span = halves * BLK

    def to(k):
        return lax.rem(me + k, groups)

    def source(k):
        return lax.rem(me - k + groups, groups)

    barrier = pltpu.get_barrier_semaphore()

    def greet(k, _):
        pl.semaphore_signal(barrier, inc=1, device_id={"lon": to(k)}, device_id_type=MESH)
        return 0

    lax.fori_loop(1, groups, greet, 0)
    inputs = []
    for b in range(halves):
        lanes = pl.ds(b * BLK, BLK)
        inputs.append(pltpu.make_async_copy(start.at[:, lanes], start_v.at[b], early.at[2 * b]))
        inputs.append(pltpu.make_async_copy(fraction.at[:, lanes], frac_v.at[b], early.at[2 * b + 1]))
    for copy in inputs:
        copy.start()
    pl.semaphore_wait(barrier, groups - 1)

    def grid_copy(a, k, peer, place):
        return pltpu.make_async_remote_copy(
            src_ref=grid.at[peer * per + a],
            dst_ref=rows[a].at[pl.ds(place * halves, halves)],
            send_sem=send1.at[a, k],
            recv_sem=recv1.at[a, k],
            device_id={"lon": peer},
            device_id_type=MESH,
        )

    def meta_copy(k, peer, place):
        return pltpu.make_async_remote_copy(
            src_ref=meta_out.at[peer],
            dst_ref=meta_in.at[place],
            send_sem=send_m.at[k],
            recv_sem=recv_m.at[k],
            device_id={"lon": peer},
            device_id_type=MESH,
        )

    def back_copy(a, k, peer, place):
        return pltpu.make_async_remote_copy(
            src_ref=moved.at[a, pl.ds(pl.multiple_of(peer * span, span), span)],
            dst_ref=departed.at[place * per + a],
            send_sem=send2.at[a, k],
            recv_sem=recv2.at[a, k],
            device_id={"lon": peer},
            device_id_type=MESH,
        )

    def send_grid(a):
        def one(k, _):
            grid_copy(a, k, to(k), me).start()
            return 0

        lax.fori_loop(1, groups, one, 0)

    def own_grid(a):
        return pltpu.make_async_copy(
            grid.at[me * per + a],
            rows[a].at[pl.ds(me * halves, halves)],
            local.at[a],
        )

    def own_back(a):
        return pltpu.make_async_copy(
            moved.at[a, pl.ds(pl.multiple_of(me * span, span), span)],
            departed.at[me * per + a],
            local.at[per + a],
        )

    send_grid(0)
    for a in range(per):
        own_grid(a).start()

    for copy in inputs:
        copy.wait()
    frac_i[...] = (frac_v[...].astype(jnp.float32) * FIX).astype(jnp.int32)

    def lay_out(t, _):
        for a in range(per):
            for b in range(halves):
                row = a * halves + b
                block = t * per * halves + row
                base = (dev[block] * halves + sub[block]) * BLK
                own = pl.ds(t * per + a, 1)
                meta_out[t, pl.ds(row, 1), :] = start_v[b, own, :] + base
                meta_out[t, pl.ds(per * halves + row, 1), :] = frac_i[b, own, :]
        return 0

    lax.fori_loop(0, groups, lay_out, 0)
    meta_in[me] = meta_out[me]

    def send_meta(k, _):
        meta_copy(k, to(k), me).start()
        return 0

    lax.fori_loop(1, groups, send_meta, 0)
    for a in range(1, per):
        send_grid(a)

    def take_meta(k, _):
        meta_copy(k, me, source(k)).wait_recv()
        return 0

    lax.fori_loop(1, groups, take_meta, 0)
    meta_copy_s = pltpu.make_async_copy(meta_in, meta_s, local.at[3 * per])
    meta_copy_s.start()
    meta_copy_s.wait()

    node = lax.broadcasted_iota(jnp.int32, (BLK, BLK), 0).astype(jnp.float32)
    lane = lax.broadcasted_iota(jnp.int32, (1, BLK), 1)

    def interpolate(a, length, t, half):
        row = a * halves + half
        j = t * halves + half
        column = meta_in[t, pl.ds(row, 1), :]
        part = meta_in[t, pl.ds(per * halves + row, 1), :].astype(jnp.float32) * (1.0 / FIX)
        begin = (column & (BLK - 1)).astype(jnp.float32)
        live = j * BLK + lane < length
        place = jnp.where(live, begin + 1.0 + part, -1000.0)
        far = jnp.abs(node - place)
        near = 2.0 - far
        inside = (1.0 - far * far) * near * 0.5
        outside = (1.0 - far) * near * (3.0 - far) * (1.0 / 6.0)
        weight = jnp.where(far < 1.0, inside, jnp.where(far < 2.0, outside, 0.0))
        upper = weight.astype(jnp.bfloat16)
        lower = (weight - upper.astype(jnp.float32)).astype(jnp.bfloat16)
        block = meta_s[t, row, 0] >> 7
        values = rows[a][block]
        total = lax.dot_general(
            jnp.concatenate([upper, lower], axis=0),
            jnp.concatenate([values, values], axis=0),
            (((0,), (0,)), ((), ())),
            preferred_element_type=jnp.float32,
        )
        result = total.astype(jnp.bfloat16)
        moved[a, pl.ds(pl.multiple_of(j * BLK, BLK), BLK), :] = result
        pieces = INNER // BLK
        wide[
            pl.ds(pl.multiple_of(lax.rem(j, pieces) * BLK, BLK), BLK),
            pl.ds(pl.multiple_of((j // pieces) * BLK, BLK), BLK),
        ] = result

    def transform(a, length):
        count = jnp.full((8, BLK), length, jnp.int32).astype(jnp.float32)
        size = jnp.broadcast_to(count[:1], (WAVES, BLK))
        inverse = 1.0 / size
        scale = 1.0 / jnp.sqrt(size)
        wave = lax.broadcasted_iota(jnp.int32, (WAVES, BLK), 0).astype(jnp.float32)
        point = lax.broadcasted_iota(jnp.int32, (WAVES, BLK), 1).astype(jnp.float32)
        first = turned(wave * point, size, inverse)
        outer = wide.shape[1] // BLK

        def one(step, _):
            base = step * WAVES
            origin = base.astype(jnp.float32)
            shift = turned(origin * point[:8], count, inverse[:8])
            shift = tuple(jnp.broadcast_to(part[:1], (WAVES, BLK)) for part in shift)
            stride = turned((origin + wave) * float(BLK), size, inverse)
            entry = times(first, shift)
            for piece in range(INNER // BLK):
                lanes = pl.ds(piece * BLK, BLK)
                table[:WAVES, lanes] = entry[0].astype(jnp.bfloat16)
                table[WAVES:, lanes] = entry[1].astype(jnp.bfloat16)
                if piece < INNER // BLK - 1:
                    entry = times(entry, stride)
            jump = stride
            for _ in range((INNER // BLK).bit_length() - 1):
                jump = times(jump, jump)
            product = jnp.dot(table[...], wide[...], preferred_element_type=jnp.float32)

            def of(h):
                part = product[:, h * BLK : (h + 1) * BLK]
                return part[:WAVES], part[WAVES:]

            total = of(outer - 1)
            for h in range(outer - 2, -1, -1):
                ahead = times(total, jump)
                here = of(h)
                total = here[0] + ahead[0], here[1] + ahead[1]
            for part in range(2):
                spectrum[a, part, pl.ds(pl.multiple_of(base, WAVES), WAVES), :] = total[part] * scale
            return 0

        lax.fori_loop(0, MMAX // WAVES, one, 0)

    def result_copy(a):
        return pltpu.make_async_copy(spectrum.at[a], fourier.at[a], local.at[2 * per + a])

    for a in range(per):
        length = npts[band * lats + me * per + a]
        own_grid(a).wait()

        def take_grid(k, _):
            grid_copy(a, k, me, source(k)).wait_recv()
            return 0

        lax.fori_loop(1, groups, take_grid, 0)
        spot = lax.broadcasted_iota(jnp.int32, (BLK, BLK), 0)
        for block in range(LEAST // BLK, rows[a].shape[0]):
            ends = rows[a][block].astype(jnp.float32)
            rows[a][block] = jnp.where(block * BLK + spot < length, ends, 0.0).astype(jnp.bfloat16)

        def answer(k, _):
            t = to(k)
            for half in range(halves):
                interpolate(a, length, t, half)
            back_copy(a, k, t, me).start()
            return 0

        lax.fori_loop(1, groups, answer, 0)
        for half in range(halves):
            interpolate(a, length, me, half)
        own_back(a).start()
        transform(a, length)
        result_copy(a).start()

    for a in range(per):
        own_back(a).wait()
        result_copy(a).wait()

        def finish(k, _):
            grid_copy(a, k, to(k), me).wait_send()
            back_copy(a, k, to(k), me).wait_send()
            back_copy(a, k, me, source(k)).wait_recv()
            return 0

        lax.fori_loop(1, groups, finish, 0)

    def finish_meta(k, _):
        meta_copy(k, to(k), me).wait_send()
        return 0

    lax.fori_loop(1, groups, finish_meta, 0)


def per_device(grid, npts, fraction, start, src_dev, src_sub):
    lats, span, channels = grid.shape
    groups = lax.axis_size("lon")
    per = lats // groups
    points = span * groups
    blocks = lats * span // BLK
    meta = (groups, 2 * per * (span // BLK), BLK)
    smem = pl.BlockSpec(memory_space=pltpu.SMEM)
    anywhere = pl.BlockSpec(memory_space=pl.ANY)
    dma = pltpu.SemaphoreType.DMA
    return pl.pallas_call(
        functools.partial(kernel, groups),
        out_shape=(
            jax.ShapeDtypeStruct(grid.shape, jnp.bfloat16),
            jax.ShapeDtypeStruct((per, 2, MMAX, channels), jnp.float32),
        ),
        in_specs=[smem, smem, smem, anywhere, anywhere, anywhere],
        out_specs=(anywhere, anywhere),
        scratch_shapes=[
            (pltpu.VMEM((points // BLK, BLK, channels), jnp.bfloat16),) * per,
            pltpu.VMEM((per, points, channels), jnp.bfloat16),
            pltpu.VMEM((INNER, points // INNER * channels), jnp.bfloat16),
            pltpu.VMEM((2 * WAVES, INNER), jnp.bfloat16),
            pltpu.VMEM((per, 2, MMAX, channels), jnp.float32),
            pltpu.VMEM((span // BLK, lats, BLK), jnp.int32),
            pltpu.VMEM((span // BLK, lats, BLK), jnp.bfloat16),
            pltpu.VMEM((span // BLK, lats, BLK), jnp.int32),
            pltpu.VMEM(meta, jnp.int32),
            pltpu.VMEM(meta, jnp.int32),
            pltpu.SMEM(meta, jnp.int32),
            dma((per, groups)),
            dma((per, groups)),
            dma((groups,)),
            dma((groups,)),
            dma((per, groups)),
            dma((per, groups)),
            dma((2 * span // BLK,)),
            dma((1 + 3 * per,)),
        ],
        compiler_params=pltpu.CompilerParams(
            collective_id=0, has_side_effects=True, vmem_limit_bytes=56 * 1024 * 1024
        ),
    )(npts, src_dev.reshape(blocks), src_sub.reshape(blocks), start, fraction, grid.reshape(lats, span // BLK, BLK, channels))


def solution(mesh):
    in_specs = (
        P("lat", "lon", None),
        P(),
        P("lat", "lon"),
        P("lat", "lon"),
        P("lat", "lon", None, None),
        P("lat", "lon", None),
    )
    out_specs = (P("lat", "lon", None), P(("lat", "lon"), None, None, None))
    return jax.shard_map(
        per_device, mesh=mesh, in_specs=in_specs, out_specs=out_specs, check_vma=False
    )
```

time: 427 us -> 110 us (0.26)
  the two profiles are of different devices: /device:TPU:65 before, /device:TPU:1 now
where the time goes in v1:
time: 110 us
  Pallas kernels  104 us (95%)
  local copies, waits for them, and re-layouts  4.78 us (4%)
    pallas_call x1, Pallas kernels, per_device(): pl.pallas_call(functools.partial(kernel, groups), out_shape=(jax.ShapeDty...  104 us
    unnamed x4, local copies, waits for them, and re-layouts  4.78 us

profile of v1, /device:TPU:1, one launch (start us, length us, event | category | flops | bytes accessed | tf_op | source)
XLA Modules:
  0.0 109.6 jit_solution(9446799010094139937)
XLA Ops:
  0.6 104.2 %shard_map.77 = (bf16[32,256,128]{2,1,0:T(8,128)(2,1)}, f32[2,2,1280,128]{3,2,1,0:T(8,128)}) custom-call(s32[512]{0:T(512)} %npts.1, s32[64]{0:T(128)} %bitcast.4, s32[64]{0:T(128)} %bitcast.5, s32[32,256]{1,0:T(8,128)} %start.1, bf16[32,256]{1,0:T(8,128)(2,1)} %fraction.1, bf16[32,2,128,128]{3,2,1,0:T(8,128)(2,1)} %bitcast.3), custom_call_target="tpu_custom_call" | custom-call | tf_op jit(solution)/shard_map/pallas_call | solution.py:325
  104.9 0.0 copy-start
  104.9 3.3 %copy.10 = bf16[32,256,128]{2,1,0:T(8,128)(2,1)} copy(bf16[32,256,128]{2,1,0:T(8,128)(2,1)} %get-tuple-element.4) | data formatting | bytes 4194304
  108.2 0.0 copy-done
  108.2 1.5 %copy.11 = f32[2,2,1280,128]{3,2,1,0:T(8,128)} copy(f32[2,2,1280,128]{3,2,1,0:T(8,128)S(1)} %copy-done) | data formatting | bytes 5242880
Async XLA Ops:
  104.9 3.3 %copy-start = (f32[2,2,1280,128]{3,2,1,0:T(8,128)S(1)}, f32[2,2,1280,128]{3,2,1,0:T(8,128)}, u32[]{:S(2)}) copy-start(f32[2,2,1280,128]{3,2,1,0:T(8,128)} %get-tuple-element.5) | copy-start | bytes 7864324

commit v2 on v1

--- a/solution.py
+++ b/solution.py
@@ -36,11 +36,22 @@
     return unit(rest * inverse)
 
 
+def answer_order(chips):
+    release = (0, 24, 33, 41, 61, 56, 47, 38)
+    codes = []
+    for z in range(chips):
+        def dist(c):
+            return min((c - z) % chips, (z - c) % chips)
+        ranked = sorted(range(chips), key=lambda c: (c == z, min(release[c], release[z]), -dist(c), (c - z) % chips))
+        codes.append(sum(c * chips**i for i, c in enumerate(ranked)))
+    return codes
+
+
 def kernel(
     groups,
-    npts,
-    dev,
-    sub,
+    npts_hbm,
+    dev_hbm,
+    sub_hbm,
     start,
     fraction,
     grid,
@@ -50,19 +61,17 @@
     moved,
     wide,
     table,
-    spectrum,
+    npts,
+    dev,
+    sub,
     start_v,
     frac_v,
     frac_i,
     meta_out,
     meta_in,
     meta_s,
-    send1,
-    recv1,
-    send_m,
-    recv_m,
-    send2,
-    recv2,
+    sent,
+    come,
     early,
     local,
 ):
@@ -76,9 +85,6 @@
     def to(k):
         return lax.rem(me + k, groups)
 
-    def source(k):
-        return lax.rem(me - k + groups, groups)
-
     barrier = pltpu.get_barrier_semaphore()
 
     def greet(k, _):
@@ -86,48 +92,54 @@
         return 0
 
     lax.fori_loop(1, groups, greet, 0)
-    inputs = []
+    inputs = [
+        pltpu.make_async_copy(far, near, early.at[2 + i])
+        for i, (far, near) in enumerate(((npts_hbm, npts), (dev_hbm, dev), (sub_hbm, sub)))
+    ]
     for b in range(halves):
         lanes = pl.ds(b * BLK, BLK)
-        inputs.append(pltpu.make_async_copy(start.at[:, lanes], start_v.at[b], early.at[2 * b]))
-        inputs.append(pltpu.make_async_copy(fraction.at[:, lanes], frac_v.at[b], early.at[2 * b + 1]))
+        inputs.append(pltpu.make_async_copy(start.at[:, lanes], start_v.at[b], early.at[0]))
+        inputs.append(pltpu.make_async_copy(fraction.at[:, lanes], frac_v.at[b], early.at[1]))
     for copy in inputs:
         copy.start()
     pl.semaphore_wait(barrier, groups - 1)
 
-    def grid_copy(a, k, peer, place):
+    def grid_copy(a, peer, place):
         return pltpu.make_async_remote_copy(
             src_ref=grid.at[peer * per + a],
             dst_ref=rows[a].at[pl.ds(place * halves, halves)],
-            send_sem=send1.at[a, k],
-            recv_sem=recv1.at[a, k],
+            send_sem=sent.at[0],
+            recv_sem=come.at[a],
             device_id={"lon": peer},
             device_id_type=MESH,
         )
 
-    def meta_copy(k, peer, place):
+    def meta_copy(peer, place):
         return pltpu.make_async_remote_copy(
             src_ref=meta_out.at[peer],
             dst_ref=meta_in.at[place],
-            send_sem=send_m.at[k],
-            recv_sem=recv_m.at[k],
+            send_sem=sent.at[1],
+            recv_sem=come.at[per],
             device_id={"lon": peer},
             device_id_type=MESH,
         )
 
-    def back_copy(a, k, peer, place):
+    def back_copy(a, peer, place):
         return pltpu.make_async_remote_copy(
             src_ref=moved.at[a, pl.ds(pl.multiple_of(peer * span, span), span)],
             dst_ref=departed.at[place * per + a],
-            send_sem=send2.at[a, k],
-            recv_sem=recv2.at[a, k],
+            send_sem=sent.at[2 + a],
+            recv_sem=come.at[per + 1],
             device_id={"lon": peer},
             device_id_type=MESH,
         )
 
+    def arrived(shape, sem):
+        pltpu.make_async_copy(shape, shape, sem).wait()
+
     def send_grid(a):
         def one(k, _):
-            grid_copy(a, k, to(k), me).start()
+            grid_copy(a, to(k), me).start()
             return 0
 
         lax.fori_loop(1, groups, one, 0)
@@ -150,7 +162,9 @@
     for a in range(per):
         own_grid(a).start()
 
-    for copy in inputs:
+    arrived(start_v, early.at[0])
+    arrived(frac_v, early.at[1])
+    for copy in inputs[:3]:
         copy.wait()
     frac_i[...] = (frac_v[...].astype(jnp.float32) * FIX).astype(jnp.int32)
 
@@ -169,19 +183,15 @@
     meta_in[me] = meta_out[me]
 
     def send_meta(k, _):
-        meta_copy(k, to(k), me).start()
+        meta_copy(to(k), me).start()
         return 0
 
     lax.fori_loop(1, groups, send_meta, 0)
     for a in range(1, per):
         send_grid(a)
 
-    def take_meta(k, _):
-        meta_copy(k, me, source(k)).wait_recv()
-        return 0
-
-    lax.fori_loop(1, groups, take_meta, 0)
-    meta_copy_s = pltpu.make_async_copy(meta_in, meta_s, local.at[3 * per])
+    arrived(meta_in.at[pl.ds(0, groups - 1)], come.at[per])
+    meta_copy_s = pltpu.make_async_copy(meta_in, meta_s, local.at[2 * per])
     meta_copy_s.start()
     meta_copy_s.wait()
 
@@ -257,59 +267,65 @@
                 here = of(h)
                 total = here[0] + ahead[0], here[1] + ahead[1]
             for part in range(2):
-                spectrum[a, part, pl.ds(pl.multiple_of(base, WAVES), WAVES), :] = total[part] * scale
+                fourier[a, part, pl.ds(pl.multiple_of(base, WAVES), WAVES), :] = total[part] * scale
             return 0
 
         lax.fori_loop(0, MMAX // WAVES, one, 0)
 
-    def result_copy(a):
-        return pltpu.make_async_copy(spectrum.at[a], fourier.at[a], local.at[2 * per + a])
+    chips = groups // 2
+    z = me // 2
+    order = jnp.int32(0)
+    for chip, code in enumerate(answer_order(chips)):
+        order = jnp.where(z == chip, code, order)
 
     for a in range(per):
         length = npts[band * lats + me * per + a]
         own_grid(a).wait()
 
-        def take_grid(k, _):
-            grid_copy(a, k, me, source(k)).wait_recv()
-            return 0
-
-        lax.fori_loop(1, groups, take_grid, 0)
+        arrived(rows[a].at[pl.ds(0, (groups - 1) * halves)], come.at[a])
         spot = lax.broadcasted_iota(jnp.int32, (BLK, BLK), 0)
         for block in range(LEAST // BLK, rows[a].shape[0]):
             ends = rows[a][block].astype(jnp.float32)
             rows[a][block] = jnp.where(block * BLK + spot < length, ends, 0.0).astype(jnp.bfloat16)
 
-        def answer(k, _):
-            t = to(k)
+        def answer(i, code):
+            t = (code % chips) * 2 + 1 - i % 2
             for half in range(halves):
                 interpolate(a, length, t, half)
-            back_copy(a, k, t, me).start()
-            return 0
-
-        lax.fori_loop(1, groups, answer, 0)
-        for half in range(halves):
-            interpolate(a, length, me, half)
-        own_back(a).start()
+
+            @pl.when(t != me)
+            def _():
+                back_copy(a, t, me).start()
+
+            @pl.when(t == me)
+            def _():
+                own_back(a).start()
+
+            return jnp.where(i % 2 == 1, code // chips, code)
+
+        lax.fori_loop(0, groups, answer, order)
         transform(a, length)
-        result_copy(a).start()
 
     for a in range(per):
         own_back(a).wait()
-        result_copy(a).wait()
-
-        def finish(k, _):
-            grid_copy(a, k, to(k), me).wait_send()
-            back_copy(a, k, to(k), me).wait_send()
-            back_copy(a, k, me, source(k)).wait_recv()
-            return 0
-
-        lax.fori_loop(1, groups, finish, 0)
-
-    def finish_meta(k, _):
-        meta_copy(k, to(k), me).wait_send()
-        return 0
-
-    lax.fori_loop(1, groups, finish_meta, 0)
+        arrived(moved.at[a, pl.ds(0, (groups - 1) * span)], sent.at[2 + a])
+    arrived(departed.at[pl.ds(0, (groups - 1) * per)], come.at[per + 1])
+    arrived(grid.at[pl.ds(0, (groups - 1) * per)], sent.at[0])
+    arrived(meta_out.at[pl.ds(0, groups - 1)], sent.at[1])
+
+
+def settle(departed, fourier, departed_out, fourier_out, sems):
+    copies = []
+    parts = sems.shape[1]
+    for i, (near, far) in enumerate(((departed, departed_out), (fourier, fourier_out))):
+        share = near.shape[0] // parts
+        for j in range(parts):
+            rows = pl.ds(j * share, share)
+            copies.append(pltpu.make_async_copy(near.at[rows], far.at[rows], sems.at[i, j]))
+    for copy in copies:
+        copy.start()
+    for copy in copies:
+        copy.wait()
 
 
 def per_device(grid, npts, fraction, start, src_dev, src_sub):
@@ -319,42 +335,60 @@
     points = span * groups
     blocks = lats * span // BLK
     meta = (groups, 2 * per * (span // BLK), BLK)
-    smem = pl.BlockSpec(memory_space=pltpu.SMEM)
-    anywhere = pl.BlockSpec(memory_space=pl.ANY)
     dma = pltpu.SemaphoreType.DMA
-    return pl.pallas_call(
+    outputs = pl.pallas_call(
         functools.partial(kernel, groups),
         out_shape=(
-            jax.ShapeDtypeStruct(grid.shape, jnp.bfloat16),
-            jax.ShapeDtypeStruct((per, 2, MMAX, channels), jnp.float32),
+            pltpu.VMEM(grid.shape, jnp.bfloat16),
+            pltpu.VMEM((per, 2, MMAX, channels), jnp.float32),
         ),
-        in_specs=[smem, smem, smem, anywhere, anywhere, anywhere],
-        out_specs=(anywhere, anywhere),
+        in_specs=[pl.BlockSpec(memory_space=pltpu.HBM)] * 6,
+        out_specs=(pl.BlockSpec(memory_space=pltpu.VMEM),) * 2,
         scratch_shapes=[
             (pltpu.VMEM((points // BLK, BLK, channels), jnp.bfloat16),) * per,
             pltpu.VMEM((per, points, channels), jnp.bfloat16),
             pltpu.VMEM((INNER, points // INNER * channels), jnp.bfloat16),
             pltpu.VMEM((2 * WAVES, INNER), jnp.bfloat16),
-            pltpu.VMEM((per, 2, MMAX, channels), jnp.float32),
+            pltpu.SMEM(npts.shape, jnp.int32),
+            pltpu.SMEM((blocks,), jnp.int32),
+            pltpu.SMEM((blocks,), jnp.int32),
             pltpu.VMEM((span // BLK, lats, BLK), jnp.int32),
             pltpu.VMEM((span // BLK, lats, BLK), jnp.bfloat16),
             pltpu.VMEM((span // BLK, lats, BLK), jnp.int32),
             pltpu.VMEM(meta, jnp.int32),
             pltpu.VMEM(meta, jnp.int32),
             pltpu.SMEM(meta, jnp.int32),
-            dma((per, groups)),
-            dma((per, groups)),
-            dma((groups,)),
-            dma((groups,)),
-            dma((per, groups)),
-            dma((per, groups)),
-            dma((2 * span // BLK,)),
-            dma((1 + 3 * per,)),
+            dma((2 + per,)),
+            dma((2 + per,)),
+            dma((5,)),
+            dma((1 + 2 * per,)),
         ],
         compiler_params=pltpu.CompilerParams(
-            collective_id=0, has_side_effects=True, vmem_limit_bytes=56 * 1024 * 1024
+            collective_id=0, has_side_effects=True, vmem_limit_bytes=24 * 1024 * 1024
         ),
-    )(npts, src_dev.reshape(blocks), src_sub.reshape(blocks), start, fraction, grid.reshape(lats, span // BLK, BLK, channels))
+    )(
+        *(
+            pltpu.with_memory_space_constraint(array, pltpu.HBM)
+            for array in (
+                npts,
+                src_dev.reshape(blocks),
+                src_sub.reshape(blocks),
+                start,
+                fraction,
+                grid.reshape(lats, span // BLK, BLK, channels),
+            )
+        ),
+    )
+    vmem = pl.BlockSpec(memory_space=pltpu.VMEM)
+    hbm = pl.BlockSpec(memory_space=pltpu.HBM)
+    return pl.pallas_call(
+        settle,
+        out_shape=tuple(pltpu.HBM(array.shape, array.dtype) for array in outputs),
+        in_specs=[vmem, vmem],
+        out_specs=(hbm, hbm),
+        scratch_shapes=[dma((2, per))],
+        compiler_params=pltpu.CompilerParams(vmem_limit_bytes=8 * 1024 * 1024),
+    )(*(pltpu.with_memory_space_constraint(array, pltpu.VMEM) for array in outputs))
 
 
 def solution(mesh):

time: 110 us -> 103 us (0.936)
  the two profiles are of different devices: /device:TPU:1 before, /device:TPU:65 now
where the time goes in v2:
time: 103 us; the launch traced here: 102 us
  Pallas kernels  101 us (98%)
    pallas_call x1, Pallas kernels, per_device(): pl.pallas_call(functools.partial(kernel, groups), out_shape=(pltpu.VMEM(g...  99.1 us
    pallas_call x1, Pallas kernels, per_device(): pl.pallas_call(settle, out_shape=tuple((pltpu.HBM(array.shape, array.dtyp...  2.22 us

profile of v2, /device:TPU:65, one launch (start us, length us, event | category | flops | bytes accessed | tf_op | source)
XLA Modules:
  0.0 101.9 jit_solution(1276531251414028401)
XLA Ops:
  0.6 99.1 %shard_map.77 = (bf16[32,256,128]{2,1,0:T(8,128)(2,1)S(1)}, f32[2,2,1280,128]{3,2,1,0:T(8,128)S(1)}) custom-call(s32[512]{0:T(512)} %npts_hbm.1, s32[64]{0:T(128)} %bitcast.4, s32[64]{0:T(128)} %bitcast.5, s32[32,256]{1,0:T(8,128)} %start.1, bf16[32,256]{1,0:T(8,128)(2,1)} %fraction.1, bf16[32,2,128,128]{3,2,1,0:T(8,128)(2,1)} %bitcast.3), custom_call_target="tpu_custom_call" | custom-call | tf_op jit(solution)/shard_map/pallas_call | solution.py:339
  99.7 2.2 %shard_map.78 = (bf16[32,256,128]{2,1,0:T(8,128)(2,1)}, f32[2,2,1280,128]{3,2,1,0:T(8,128)}) custom-call(bf16[32,256,128]{2,1,0:T(8,128)(2,1)S(1)} %get-tuple-element.4.departed, f32[2,2,1280,128]{3,2,1,0:T(8,128)S(1)} %get-tuple-element.5.fourier), custom_call_target="tpu_custom_call" | custom-call | tf_op jit(solution)/shard_map/pallas_call | solution.py:384

commit v3 on v2

--- a/solution.py
+++ b/solution.py
@@ -13,7 +13,7 @@
 WAVES = 128
 INNER = 512
 LEAST = 3328
-FIX = float(1 << 24)
+FIX = (1 << 16) - 1
 MESH = pl.DeviceIdType.MESH
 
 
@@ -37,13 +37,18 @@
 
 
 def answer_order(chips):
-    release = (0, 24, 33, 41, 61, 56, 47, 38)
+    ranks = [min(c, chips - c, chips // 4) for c in range(chips)]
+    ranks[1:chips // 4 + 1] = [1] * (chips // 4)
     codes = []
-    for z in range(chips):
-        def dist(c):
-            return min((c - z) % chips, (z - c) % chips)
-        ranked = sorted(range(chips), key=lambda c: (c == z, min(release[c], release[z]), -dist(c), (c - z) % chips))
-        codes.append(sum(c * chips**i for i, c in enumerate(ranked)))
+    for device in range(2 * chips):
+        z, by_reader = device // 2, device % 2 == 1
+
+        def key(c):
+            hops = min((c - z) % chips, (z - c) % chips)
+            rank = ranks[c] if by_reader else min(ranks[c], ranks[z])
+            return c == z, rank, -hops, (c - z) % chips
+
+        codes.append(sum(c * chips**i for i, c in enumerate(sorted(range(chips), key=key))))
     return codes
 
 
@@ -166,7 +171,7 @@
     arrived(frac_v, early.at[1])
     for copy in inputs[:3]:
         copy.wait()
-    frac_i[...] = (frac_v[...].astype(jnp.float32) * FIX).astype(jnp.int32)
+    frac_i[...] = (frac_v[...].astype(jnp.float32) * float(FIX) + 0.5).astype(jnp.int32) & FIX
 
     def lay_out(t, _):
         for a in range(per):
@@ -175,8 +180,7 @@
                 block = t * per * halves + row
                 base = (dev[block] * halves + sub[block]) * BLK
                 own = pl.ds(t * per + a, 1)
-                meta_out[t, pl.ds(row, 1), :] = start_v[b, own, :] + base
-                meta_out[t, pl.ds(per * halves + row, 1), :] = frac_i[b, own, :]
+                meta_out[t, pl.ds(row, 1), :] = (start_v[b, own, :] + base) * (FIX + 1) + frac_i[b, own, :]
         return 0
 
     lax.fori_loop(0, groups, lay_out, 0)
@@ -201,9 +205,9 @@
     def interpolate(a, length, t, half):
         row = a * halves + half
         j = t * halves + half
-        column = meta_in[t, pl.ds(row, 1), :]
-        part = meta_in[t, pl.ds(per * halves + row, 1), :].astype(jnp.float32) * (1.0 / FIX)
-        begin = (column & (BLK - 1)).astype(jnp.float32)
+        word = meta_in[t, pl.ds(row, 1), :]
+        part = (word & FIX).astype(jnp.float32) * (1.0 / FIX)
+        begin = ((word >> 16) & (BLK - 1)).astype(jnp.float32)
         live = j * BLK + lane < length
         place = jnp.where(live, begin + 1.0 + part, -1000.0)
         far = jnp.abs(node - place)
@@ -213,7 +217,7 @@
         weight = jnp.where(far < 1.0, inside, jnp.where(far < 2.0, outside, 0.0))
         upper = weight.astype(jnp.bfloat16)
         lower = (weight - upper.astype(jnp.float32)).astype(jnp.bfloat16)
-        block = meta_s[t, row, 0] >> 7
+        block = jnp.clip(meta_s[t, row, 0] >> 23, 0, rows[a].shape[0] - 1)
         values = rows[a][block]
         total = lax.dot_general(
             jnp.concatenate([upper, lower], axis=0),
@@ -273,10 +277,9 @@
         lax.fori_loop(0, MMAX // WAVES, one, 0)
 
     chips = groups // 2
-    z = me // 2
     order = jnp.int32(0)
-    for chip, code in enumerate(answer_order(chips)):
-        order = jnp.where(z == chip, code, order)
+    for device, code in enumerate(answer_order(chips)):
+        order = jnp.where(me == device, code, order)
 
     for a in range(per):
         length = npts[band * lats + me * per + a]
@@ -289,7 +292,7 @@
             rows[a][block] = jnp.where(block * BLK + spot < length, ends, 0.0).astype(jnp.bfloat16)
 
         def answer(i, code):
-            t = (code % chips) * 2 + 1 - i % 2
+            t = (code % chips) * 2 + lax.rem(i + me, 2)
             for half in range(halves):
                 interpolate(a, length, t, half)
 
@@ -334,7 +337,7 @@
     per = lats // groups
     points = span * groups
     blocks = lats * span // BLK
-    meta = (groups, 2 * per * (span // BLK), BLK)
+    meta = (groups, per * (span // BLK), BLK)
     dma = pltpu.SemaphoreType.DMA
     outputs = pl.pallas_call(
         functools.partial(kernel, groups),

time: 103 us -> 103 us (level)
  no operation moved by 1% of the time
where the time goes in v3:
time: 103 us; the launch traced here: 102 us
  Pallas kernels  101 us (98%)
    pallas_call x1, Pallas kernels, per_device(): pl.pallas_call(functools.partial(kernel, groups), out_shape=(pltpu.VMEM(g...  98.9 us
    pallas_call x1, Pallas kernels, per_device(): pl.pallas_call(settle, out_shape=tuple((pltpu.HBM(array.shape, array.dtyp...  2.22 us

profile of v3, /device:TPU:65, one launch (start us, length us, event | category | flops | bytes accessed | tf_op | source)
XLA Modules:
  0.0 101.8 jit_solution(9573082445869082127)
XLA Ops:
  0.6 98.9 %shard_map.77 = (bf16[32,256,128]{2,1,0:T(8,128)(2,1)S(1)}, f32[2,2,1280,128]{3,2,1,0:T(8,128)S(1)}) custom-call(s32[512]{0:T(512)} %npts_hbm.1, s32[64]{0:T(128)} %bitcast.4, s32[64]{0:T(128)} %bitcast.5, s32[32,256]{1,0:T(8,128)} %start.1, bf16[32,256]{1,0:T(8,128)(2,1)} %fraction.1, bf16[32,2,128,128]{3,2,1,0:T(8,128)(2,1)} %bitcast.3), custom_call_target="tpu_custom_call" | custom-call | tf_op jit(solution)/shard_map/pallas_call | solution.py:342
  99.6 2.2 %shard_map.78 = (bf16[32,256,128]{2,1,0:T(8,128)(2,1)}, f32[2,2,1280,128]{3,2,1,0:T(8,128)}) custom-call(bf16[32,256,128]{2,1,0:T(8,128)(2,1)S(1)} %get-tuple-element.4.departed, f32[2,2,1280,128]{3,2,1,0:T(8,128)S(1)} %get-tuple-element.5.fourier), custom_call_target="tpu_custom_call" | custom-call | tf_op jit(solution)/shard_map/pallas_call | solution.py:387

commit v4 on v3

--- a/solution.py
+++ b/solution.py
@@ -37,8 +37,7 @@
 
 
 def answer_order(chips):
-    ranks = [min(c, chips - c, chips // 4) for c in range(chips)]
-    ranks[1:chips // 4 + 1] = [1] * (chips // 4)
+    ranks = [min(c, 3) for c in range(chips)]
     codes = []
     for device in range(2 * chips):
         z, by_reader = device // 2, device % 2 == 1

time: 103 us -> 102 us (level); the launches traced: 102 us -> 102 us
  no operation moved by 1% of the time
where the time goes in v4:
time: 102 us
  Pallas kernels  101 us (99%)
    pallas_call x1, Pallas kernels, per_device(): pl.pallas_call(functools.partial(kernel, groups), out_shape=(pltpu.VMEM(g...  99 us
    pallas_call x1, Pallas kernels, per_device(): pl.pallas_call(settle, out_shape=tuple((pltpu.HBM(array.shape, array.dtyp...  2.22 us

profile of v4, /device:TPU:65, one launch (start us, length us, event | category | flops | bytes accessed | tf_op | source)
XLA Modules:
  0.0 101.9 jit_solution(18305876657989902522)
XLA Ops:
  0.6 99.0 %shard_map.77 = (bf16[32,256,128]{2,1,0:T(8,128)(2,1)S(1)}, f32[2,2,1280,128]{3,2,1,0:T(8,128)S(1)}) custom-call(s32[512]{0:T(512)} %npts_hbm.1, s32[64]{0:T(128)} %bitcast.4, s32[64]{0:T(128)} %bitcast.5, s32[32,256]{1,0:T(8,128)} %start.1, bf16[32,256]{1,0:T(8,128)(2,1)} %fraction.1, bf16[32,2,128,128]{3,2,1,0:T(8,128)(2,1)} %bitcast.3), custom_call_target="tpu_custom_call" | custom-call | tf_op jit(solution)/shard_map/pallas_call | solution.py:341
  99.7 2.2 %shard_map.78 = (bf16[32,256,128]{2,1,0:T(8,128)(2,1)}, f32[2,2,1280,128]{3,2,1,0:T(8,128)}) custom-call(bf16[32,256,128]{2,1,0:T(8,128)(2,1)S(1)} %get-tuple-element.4.departed, f32[2,2,1280,128]{3,2,1,0:T(8,128)S(1)} %get-tuple-element.5.fourier), custom_call_target="tpu_custom_call" | custom-call | tf_op jit(solution)/shard_map/pallas_call | solution.py:386

commit v5 on v4

--- a/solution.py
+++ b/solution.py
@@ -37,7 +37,7 @@
 
 
 def answer_order(chips):
-    ranks = [min(c, 3) for c in range(chips)]
+    ranks = [0, 1, 2, 3, 3, 3, 3, 2]
     codes = []
     for device in range(2 * chips):
         z, by_reader = device // 2, device % 2 == 1

time: 102 us -> 102 us (level)
  no operation moved by 1% of the time
where the time goes in v5:
time: 102 us
  Pallas kernels  101 us (99%)
    pallas_call x1, Pallas kernels, per_device(): pl.pallas_call(functools.partial(kernel, groups), out_shape=(pltpu.VMEM(g...  99 us
    pallas_call x1, Pallas kernels, per_device(): pl.pallas_call(settle, out_shape=tuple((pltpu.HBM(array.shape, array.dtyp...  2.22 us

profile of v5, /device:TPU:65, one launch (start us, length us, event | category | flops | bytes accessed | tf_op | source)
XLA Modules:
  0.0 101.9 jit_solution(9381869526924432743)
XLA Ops:
  0.6 99.0 %shard_map.77 = (bf16[32,256,128]{2,1,0:T(8,128)(2,1)S(1)}, f32[2,2,1280,128]{3,2,1,0:T(8,128)S(1)}) custom-call(s32[512]{0:T(512)} %npts_hbm.1, s32[64]{0:T(128)} %bitcast.4, s32[64]{0:T(128)} %bitcast.5, s32[32,256]{1,0:T(8,128)} %start.1, bf16[32,256]{1,0:T(8,128)(2,1)} %fraction.1, bf16[32,2,128,128]{3,2,1,0:T(8,128)(2,1)} %bitcast.3), custom_call_target="tpu_custom_call" | custom-call | tf_op jit(solution)/shard_map/pallas_call | solution.py:341
  99.7 2.2 %shard_map.78 = (bf16[32,256,128]{2,1,0:T(8,128)(2,1)}, f32[2,2,1280,128]{3,2,1,0:T(8,128)}) custom-call(bf16[32,256,128]{2,1,0:T(8,128)(2,1)S(1)} %get-tuple-element.4.departed, f32[2,2,1280,128]{3,2,1,0:T(8,128)S(1)} %get-tuple-element.5.fourier), custom_call_target="tpu_custom_call" | custom-call | tf_op jit(solution)/shard_map/pallas_call | solution.py:386
